TPU v7x, 256 devices: a whole 4x4x8 slice. The times are simulated.
256 devices in a mesh: silo: 16 (over y, x), feat: 16 (over z, core).
Axes of the slice: x: 4, y: 4, z: 8, core: 2. Of those that a mesh axis runs over, the one named last changes fastest.
Arguments:
- samples: bfloat16 [8192, 131072], P('silo', 'feat'), may hold values from -6 to 6
- components: bfloat16 [64, 131072], P(None, 'feat'), may hold values from -0.015625 to 0.015625
- row_counts: int32 [16], P('silo'), may hold values from 128 to 512, as said below
- observed: int32 [16, 256], P('silo', 'feat'), may hold values from 0 to 1, as said below
- block_owner: int32 [256], P('feat'), may hold values from 0 to 15, as said below
Outputs:
- grad_owned: float32 [64, 131072], P(None, ('silo', 'feat'))
Inputs may be any that keep to these rules, and one draw needn't show every extreme that they name: `row_counts`: one silo has all 512 row slots used in every draw. `observed`: every entry is 0 or 1, and at least one entry is 1 (some silo observes some block). `block_owner`: each silo owns exactly 1 block of every slice of 16 blocks.
All inputs are finite; a program needn't handle non-finite values.
Results may differ from a plain program's by a relative error of at most 0.0029.
Values sent between devices are 32-bit elements; how exact they have to be, the bound alone decides.
A program may use at most 64 MiB of HBM per device.

v0:
```python
import jax
import jax.numpy as jnp
from jax import lax
from jax.sharding import PartitionSpec as P


def local(samples, components, row_counts, observed, block_owner):
    num_rows, num_feat = samples.shape
    num_comp = components.shape[0]
    num_blocks = block_owner.shape[0]
    blk_width = num_feat // num_blocks
    num_silos = lax.axis_size("silo")
    own_count = num_blocks // num_silos
    col_mask = jnp.repeat(observed[0], blk_width).astype(jnp.bfloat16)
    masked_comp = components * col_mask[None, :]
    proj_part = jnp.einsum("rf,kf->rk", samples, masked_comp, preferred_element_type=jnp.float32)
    gram_part = jnp.einsum("kf,jf->kj", components, components, preferred_element_type=jnp.float32)
    projected, gram_matrix = lax.psum((proj_part, gram_part), "feat")
    row_mask = (jnp.arange(num_rows, dtype=jnp.int32) < row_counts[0]).astype(jnp.float32)
    projected = projected * row_mask[:, None]
    proj_bf = projected.astype(jnp.bfloat16)
    partial_value = jnp.einsum("rk,rf->kf", proj_bf, samples, preferred_element_type=jnp.float32)
    partial_value = partial_value * col_mask[None, :].astype(jnp.float32)
    cross_part = jnp.einsum("rk,rj->kj", projected, projected, precision=lax.Precision.HIGHEST)
    cross_sum, row_total = lax.psum((cross_part, row_counts[0].astype(jnp.float32)), "silo")
    block_idx = jnp.arange(num_blocks, dtype=jnp.int32)
    arrange_order = jnp.argsort(block_owner * num_blocks + block_idx)
    my_silo = lax.axis_index("silo")
    my_blocks = lax.dynamic_slice_in_dim(arrange_order, my_silo * own_count, own_count)
    comp_own = jnp.take(components.reshape(num_comp, num_blocks, blk_width), my_blocks, axis=1)
    comp_own = comp_own.reshape(num_comp, own_count * blk_width).astype(jnp.float32)
    arranged = jnp.take(
        partial_value.reshape(num_comp, num_blocks, blk_width), arrange_order, axis=1
    )
    arranged = arranged.reshape(num_comp, num_feat)
    summed = lax.psum_scatter(arranged, "silo", scatter_dimension=1, tiled=True)
    factor = 2.0 * jnp.eye(num_comp, dtype=jnp.float32) - gram_matrix
    gradient = jnp.dot(factor, summed, precision=lax.Precision.HIGHEST) - jnp.dot(
        cross_sum, comp_own, precision=lax.Precision.HIGHEST
    )
    return -2.0 / row_total * gradient


def solution(mesh):
    in_specs = (P("silo", "feat"), P(None, "feat"), P("silo"), P("silo", "feat"), P("feat"))
    out_specs = P(None, ("silo", "feat"))
    return jax.shard_map(local, mesh=mesh, in_specs=in_specs, out_specs=out_specs, check_vma=False)
```

profile of v0, /device:TPU:32, one launch (start us, length us, event | category | flops | bytes accessed | tf_op | source)
XLA Modules:
  0.0 269.4 jit_solution(14465284576868919701)
XLA Ops:
  6.5 0.7 convert_bitcast_fusion
  7.2 0.1 broadcast_bitcast_fusion.1
  7.3 7.0 %convolution_bitcast_fusion = f32[512,64]{0,1:T(8,128)} fusion(bf16[512,8192]{1,0:T(8,128)(2,1)} %param.5, bf16[64,8192]{1,0:T(8,128)(2,1)} %param.6, bf16[8192]{0:T(1024)(128)(2,1)S(1)} %bitcast.39), kind=kOutput, calls=%fused_computation.5 | convolution fusion | flops 537395200 | bytes 9584640 | tf_op jit(solution)/shard_map/rf,kf->rk/dot_general | solution.py:16
  14.3 0.0 all-reduce.3.cloned.1.call-update
  14.4 0.0 reduce-scatter.2.cloned.1.call-start
  14.5 1.3 sort.17
  16.5 0.1 broadcast_bitcast_fusion
  16.6 105.5 %all-reduce.3.cloned.1.call-done = f32[512,64]{0,1:T(8,128)} async-done(((f32[512,64]{0,1:T(8,128)}), f32[512,64]{0,1:T(8,128)}) %all-reduce.3.cloned.1.call-update) | async-done | bytes 131088 | tf_op jit(solution)/shard_map/psum | solution.py:18
  122.1 5.0 %convolution_multiply_fusion = f32[64,8192]{1,0:T(8,128)S(1)} fusion(bf16[512,8192]{1,0:T(8,128)(2,1)} %param.5, f32[8192]{0:T(1024)S(1)} %convert_element_type.46, f32[512,64]{0,1:T(8,128)} %all-reduce.3.cloned.1.call-done, f32[512]{0:T(512)S(1)} %fusion.14), kind=kOutput, calls=%fused_computation.1 | convolution fusion | flops 537460736 | bytes 10651648 | tf_op jit(solution)/shard_map/rk,rf->kf/dot_general | solution.py:22
  127.1 0.2 copy.20
  127.3 2.0 gather_fusion
  129.4 1.8 copy.11
  131.2 1.5 broadcast_select_fusion
  132.7 0.0 reduce-scatter.2.cloned.1.call-update
  132.7 0.6 dynamic_slice.3
  135.3 0.4 copy.14
  135.6 0.4 fusion.17
  136.0 48.5 %psum.29 = f32[64,64]{1,0:T(8,128)S(1)} all-reduce(f32[64,64]{1,0:T(8,128)S(1)} %fusion.17), channel_id=1, replica_groups=mesh['silo'=16,'feat'=16] {'feat'}, use_global_device_ids=true, to_apply=%region_1.0 | all-reduce | flops 4096 | bytes 32768 | tf_op jit(solution)/shard_map/psum | solution.py:18
  184.5 0.2 broadcast_select_fusion.1
  184.7 0.3 fusion.3
  185.0 74.8 %all-reduce = (f32[64,64]{1,0:T(8,128)S(1)}, f32[]{:T(128)}) all-reduce(f32[64,64]{1,0:T(8,128)S(1)} %fusion.3, f32[]{:T(128)S(6)} %convert_element_type.40), channel_id=1, replica_groups=mesh['silo'=16,'feat'=16] {'silo'}, use_global_device_ids=true, to_apply=%region_5.6 | all-reduce | flops 4097 | bytes 32776 | tf_op jit(solution)/shard_map/psum | solution.py:25
  260.5 0.2 fusion.5
  260.7 0.0 reduce-scatter.2.cloned.1.call-done
  260.7 1.8 fusion
  (16 shorter events, 0.1 us)
Async XLA Ops:
  6.5 115.6 %all-reduce.3.cloned.1.call-start = ((), (), s32[]{:S(2)}) async-start(), calls=%async_computation.1 | async-start | bytes 262144 | tf_op jit(solution)/shard_map/psum | solution.py:18
  7.3 7.1 %copy-start.2 = (s32[16]{0:T(128)S(1)}, s32[16]{0:T(128)}, u32[]{:S(2)}) copy-start(s32[16]{0:T(128)} %param.9) | copy-start | bytes 196
  14.4 246.3 %reduce-scatter.2.cloned.1.call-start = ((), (), s32[]{:S(2)}) async-start(), calls=%async_computation.2 | async-start | bytes 2228224 | tf_op jit(solution)/shard_map/reduce_scatter | solution.py:36
  132.7 2.6 copy-start
  135.3 49.5 %copy-start.1 = (f32[512,64]{0,1:T(8,128)S(1)}, f32[512,64]{0,1:T(8,128)}, u32[]{:S(2)}) copy-start(f32[512,64]{0,1:T(8,128)} %all-reduce.3.cloned.1.call-done) | copy-start | bytes 393220
Sparse Core Ops, SparseCore 0:
  14.5 107.5 all-reduce.2
  132.8 82.1 reduce-scatter.1
where the time goes:
time: 271 us; the launch traced here: 269 us
  blocking collectives  123 us (45%)
  waiting for transfers between devices  106 us (39%)
  between operations  16.9 us (6%)
  matrix products  14.8 us (5%)
  local copies, waits for them, and re-layouts  5.16 us (2%)
  other arithmetic  3.7 us (1%)
    psum x1, waiting for transfers between devices, local(): projected, gram_matrix = lax.psum((proj_part, gram_part), 'feat')  106 us
    psum x1, blocking collectives, local(): lax.psum((cross_part, row_counts[0].astype(jnp.float32)), 'silo')  74.8 us
    psum x1, blocking collectives, local(): projected, gram_matrix = lax.psum((proj_part, gram_part), 'feat')  48.5 us
    dot_general x1, matrix products, local(): jnp.einsum('rf,kf->rk', samples, masked_comp, preferred_element_type=jnp....  7.04 us
  transfers between devices with their start and end apart: 2, of which 1 were waited for; matrix products, arithmetic and copies ran while one was open for 1% of the time, Pallas kernels for 0%

commit v1 on v0

v1 whole, which is shorter than its diff:
```python
import jax
import jax.numpy as jnp
from jax import lax
from jax.experimental import pallas as pl
from jax.experimental.pallas import tpu as pltpu
from jax.sharding import PartitionSpec as P

MESH = pl.DeviceIdType.MESH
F32 = jnp.float32
BF16 = jnp.bfloat16
HIGHEST = lax.Precision.HIGHEST
SIDE = 4
NF = 16
NB = 16
W = 512
HALF = 256
ROWS = 512
K = 64
CH = 18


def dot_nt(a, b, precision=None):
    return lax.dot_general(
        a, b, (((1,), (1,)), ((), ())), precision=precision, preferred_element_type=F32
    )


def dot_nn(a, b):
    return jnp.dot(a, b, preferred_element_type=F32)


def dot_tn(a, b, precision=None):
    return lax.dot_general(
        a, b, (((0,), (0,)), ((), ())), precision=precision, preferred_element_type=F32
    )


def kernel(
    samples, components, counts, observed, owner, out,
    xv, acc, sbuf, r1, g2, gp, inv, lhs, lhs_c, cnt, cnt_r,
    ta, tb, ra, rb, sa, sb, r2a, r2b,
    ld_sem, s1_s, s1_r, s2_s, s2_r, c_s, c_r,
    a1_s, a1_r, b1_s, b1_r, a2_s, a2_r, b2_s, b2_r,
):
    silo = lax.axis_index("silo")
    f = lax.axis_index("feat")
    y, x = silo // SIDE, silo % SIDE

    def feat_dev(off):
        return (silo, lax.rem(f + off, NF))

    def silo_dev(dy, dx):
        return (lax.rem(y + dy, SIDE) * SIDE + lax.rem(x + dx, SIDE), f)

    def loads(b):
        cols = pl.ds(pl.multiple_of(b * W, W), W)
        return (
            pltpu.make_async_copy(samples.at[:, cols], xv.at[b, pl.ds(0, ROWS)], ld_sem.at[b, 0]),
            pltpu.make_async_copy(components.at[:, cols], xv.at[b, pl.ds(ROWS, K)], ld_sem.at[b, 1]),
            pltpu.make_async_copy(components.at[:, cols], xv.at[b, pl.ds(ROWS + K, K)], ld_sem.at[b, 2]),
        )

    barrier = pltpu.get_barrier_semaphore()
    for off in range(1, NF):
        pl.semaphore_signal(barrier, inc=1, device_id=feat_dev(off), device_id_type=MESH)
    for k in range(1, SIDE):
        pl.semaphore_signal(barrier, inc=1, device_id=silo_dev(0, k), device_id_type=MESH)
        pl.semaphore_signal(barrier, inc=1, device_id=silo_dev(k, 0), device_id_type=MESH)

    def start_load(b, c):
        for cp in loads(b):
            cp.start()
        return c

    lax.fori_loop(0, NB, start_load, 0)

    def invert(d, c):
        total = jnp.int32(0)
        for b in range(NB):
            total = jnp.where(owner[b] == d, jnp.int32(b), total)
        inv[d] = total
        return c

    lax.fori_loop(0, NB, invert, 0)
    cnt[0] = jnp.full((8, 128), counts[0].astype(F32), F32)

    acc[...] = jnp.zeros_like(acc)
    left = lax.broadcasted_iota(jnp.int32, (HALF, 128), 1) < K
    left_g = lax.broadcasted_iota(jnp.int32, (32, 128), 1) < K

    def project(b, c):
        for cp in loads(b):
            cp.wait()
        seen = observed[0, b].astype(F32)
        r = dot_nt(xv[b, 0 : ROWS + K, :], xv[b, ROWS : ROWS + 2 * K, :])
        acc[0:HALF, :] += seen * jnp.where(left, r[0:HALF], r[HALF:ROWS])
        acc[HALF : HALF + 32, :] += jnp.where(
            left_g, r[ROWS : ROWS + 32], r[ROWS + 32 : ROWS + 64]
        )
        return c

    lax.fori_loop(0, NB, project, 0)

    for j in range(NF):
        sbuf[j, 0:16, :] = acc[16 * j : 16 * j + 16, :]
        sbuf[j, 16:18, :] = acc[HALF + 2 * j : HALF + 2 * j + 2, :]

    pl.semaphore_wait(barrier, NF - 1 + 2 * (SIDE - 1))

    def rs_copy(off):
        peer = lax.rem(f + off, NF)
        return pltpu.make_async_remote_copy(
            src_ref=sbuf.at[peer], dst_ref=r1.at[off], send_sem=s1_s.at[off],
            recv_sem=s1_r.at[off], device_id=(silo, peer), device_id_type=MESH,
        )

    order = [8, 9, 7, 6, 10, 11, 5, 4, 12, 13, 3, 2, 14, 15, 1]
    for off in order:
        rs_copy(off).start()

    def cnt_copy(k, stage):
        dev = silo_dev(0, k) if stage == 0 else silo_dev(k, 0)
        return pltpu.make_async_remote_copy(
            src_ref=cnt.at[stage], dst_ref=cnt_r.at[stage, k], send_sem=c_s.at[stage, k],
            recv_sem=c_r.at[stage, k], device_id=dev, device_id_type=MESH,
        )

    for k in range(1, SIDE):
        cnt_copy(k, 0).start()

    total = sbuf[f]
    for off in range(1, NF):
        rs_copy(off).wait_recv()
        total = total + r1[off]
    g2[f] = total

    def ag_copy(off):
        return pltpu.make_async_remote_copy(
            src_ref=g2.at[f], dst_ref=g2.at[f], send_sem=s2_s.at[off],
            recv_sem=s2_r.at[off], device_id=feat_dev(off), device_id_type=MESH,
        )

    for off in order:
        ag_copy(off).start()

    for k in range(1, SIDE):
        cnt_copy(k, 0).wait_recv()
    cnt[1] = cnt[0] + cnt_r[0, 1] + cnt_r[0, 2] + cnt_r[0, 3]
    for k in range(1, SIDE):
        cnt_copy(k, 1).start()

    for off in range(1, NF):
        ag_copy(off).wait_recv()

    used = counts[0]
    lane = lax.broadcasted_iota(jnp.int32, (HALF, 128), 1)
    row = lax.broadcasted_iota(jnp.int32, (HALF, 128), 0)
    row = row + jnp.where(lane >= K, HALF, 0)
    proj = g2[:, 0:16, :].reshape(HALF, 128)
    proj = jnp.where(row < used, proj, 0.0)
    for j in range(NF):
        gp[2 * j : 2 * j + 2, :] = g2[j, 16:18, :]
    gram = gp[...]
    gram_r = pltpu.roll(gram, K, 1)
    zero = jnp.zeros_like(gram)
    factor = jnp.concatenate(
        [
            jnp.where(left_g, gram, zero), jnp.where(left_g, gram_r, zero),
            jnp.where(left_g, zero, gram_r), jnp.where(left_g, zero, gram),
        ],
        axis=0,
    )
    r_i = lax.broadcasted_iota(jnp.int32, (128, 128), 0)
    c_i = lax.broadcasted_iota(jnp.int32, (128, 128), 1)
    factor = jnp.where(r_i == c_i, 2.0, 0.0) - factor
    q = dot_nt(factor, proj.astype(BF16).astype(F32), HIGHEST)
    q_hi = q.astype(BF16)
    q_lo = (q - q_hi.astype(F32)).astype(BF16)
    lhs[0:K, 0:HALF] = q_hi[0:K]
    lhs[K : 2 * K, 0:HALF] = q_lo[0:K]
    lhs[0:K, HALF:ROWS] = q_hi[K : 2 * K]
    lhs[K : 2 * K, HALF:ROWS] = q_lo[K : 2 * K]
    cross = dot_tn(proj, proj, HIGHEST)
    left_k = lax.broadcasted_iota(jnp.int32, (K, 128), 1) < K
    top, bottom = cross[0:K], cross[K : 2 * K]
    cross = jnp.where(left_k, top, bottom) + jnp.where(
        left_k, pltpu.roll(bottom, K, 1), pltpu.roll(top, K, 1)
    )
    c_hi = cross.astype(BF16).astype(F32)
    c_lo = cross - c_hi
    lhs_c[...] = jnp.where(left_k, -c_hi, -c_lo).astype(BF16)

    def half_block(dy, dx, cols):
        d = lax.rem(y + dy, SIDE) * SIDE + lax.rem(x + dx, SIDE)
        b = inv[d]
        seen = observed[0, b].astype(F32)
        p = dot_nn(lhs[...], xv[b, 0:ROWS, cols])
        return seen * (p[0:K] + p[K : 2 * K]) + dot_nn(
            lhs_c[...], xv[b, ROWS : ROWS + 2 * K, cols]
        )

    ca, cb = slice(0, HALF), slice(HALF, W)

    def a1_copy(k, i):
        return pltpu.make_async_remote_copy(
            src_ref=ta.at[k, i], dst_ref=ra.at[k, i], send_sem=a1_s.at[k, i],
            recv_sem=a1_r.at[k, i], device_id=silo_dev(0, k), device_id_type=MESH,
        )

    def b1_copy(k, i):
        return pltpu.make_async_remote_copy(
            src_ref=tb.at[k, i], dst_ref=rb.at[k, i], send_sem=b1_s.at[k, i],
            recv_sem=b1_r.at[k, i], device_id=silo_dev(k, 0), device_id_type=MESH,
        )

    def first(n, c):
        k = lax.rem(n // SIDE + 1, SIDE - 1) + 1
        i = lax.rem(n, SIDE)
        ta[k, i] = half_block(i, k, ca)
        a1_copy(k, i).start()
        tb[k, i] = half_block(k, i, cb)
        b1_copy(k, i).start()
        return c

    lax.fori_loop(0, SIDE * (SIDE - 1), first, 0)

    def own(i, c):
        ta[0, i] = half_block(i, 0, ca)
        tb[0, i] = half_block(0, i, cb)
        return c

    lax.fori_loop(0, SIDE, own, 0)

    def a2_copy(k):
        return pltpu.make_async_remote_copy(
            src_ref=sa.at[k], dst_ref=r2a.at[k], send_sem=a2_s.at[k],
            recv_sem=a2_r.at[k], device_id=silo_dev(k, 0), device_id_type=MESH,
        )

    def b2_copy(k):
        return pltpu.make_async_remote_copy(
            src_ref=sb.at[k], dst_ref=r2b.at[k], send_sem=b2_s.at[k],
            recv_sem=b2_r.at[k], device_id=silo_dev(0, k), device_id_type=MESH,
        )

    for i in (2, 3, 1, 0):
        for k in range(1, SIDE):
            a1_copy(k, i).wait_recv()
        sa[i] = ta[0, i] + ra[1, i] + ra[2, i] + ra[3, i]
        if i:
            a2_copy(i).start()
        for k in range(1, SIDE):
            b1_copy(k, i).wait_recv()
        sb[i] = tb[0, i] + rb[1, i] + rb[2, i] + rb[3, i]
        if i:
            b2_copy(i).start()

    for k in range(1, SIDE):
        cnt_copy(k, 1).wait_recv()
    rows = cnt[1] + cnt_r[1, 1] + cnt_r[1, 2] + cnt_r[1, 3]
    scale = -2.0 / rows[0:1, 0:1]
    for k in range(1, SIDE):
        a2_copy(k).wait_recv()
        b2_copy(k).wait_recv()
    out[:, 0:HALF] = scale * (sa[0] + r2a[1] + r2a[2] + r2a[3])
    out[:, HALF:W] = scale * (sb[0] + r2b[1] + r2b[2] + r2b[3])

    for off in range(1, NF):
        rs_copy(off).wait_send()
        ag_copy(off).wait_send()
    for k in range(1, SIDE):
        cnt_copy(k, 0).wait_send()
        cnt_copy(k, 1).wait_send()
        a2_copy(k).wait_send()
        b2_copy(k).wait_send()
        for i in range(SIDE):
            a1_copy(k, i).wait_send()
            b1_copy(k, i).wait_send()


def local(samples, components, row_counts, observed, block_owner):
    dma = pltpu.SemaphoreType.DMA
    return pl.pallas_call(
        kernel,
        name="pca_grad",
        out_shape=jax.ShapeDtypeStruct((K, W), F32),
        in_specs=[
            pl.BlockSpec(memory_space=pl.ANY),
            pl.BlockSpec(memory_space=pl.ANY),
            pl.BlockSpec(memory_space=pltpu.SMEM),
            pl.BlockSpec(memory_space=pltpu.SMEM),
            pl.BlockSpec(memory_space=pltpu.SMEM),
        ],
        out_specs=pl.BlockSpec(memory_space=pltpu.VMEM),
        scratch_shapes=[
            pltpu.VMEM((NB, ROWS + 2 * K, W), BF16),
            pltpu.VMEM((HALF + 32, 128), F32),
            pltpu.VMEM((NF, CH, 128), F32),
            pltpu.VMEM((NF, CH, 128), F32),
            pltpu.VMEM((NF, CH, 128), F32),
            pltpu.VMEM((32, 128), F32),
            pltpu.SMEM((NB,), jnp.int32),
            pltpu.VMEM((2 * K, ROWS), BF16),
            pltpu.VMEM((K, 128), BF16),
            pltpu.VMEM((2, 8, 128), F32),
            pltpu.VMEM((2, SIDE, 8, 128), F32),
            pltpu.VMEM((SIDE, SIDE, K, HALF), F32),
            pltpu.VMEM((SIDE, SIDE, K, HALF), F32),
            pltpu.VMEM((SIDE, SIDE, K, HALF), F32),
            pltpu.VMEM((SIDE, SIDE, K, HALF), F32),
            pltpu.VMEM((SIDE, K, HALF), F32),
            pltpu.VMEM((SIDE, K, HALF), F32),
            pltpu.VMEM((SIDE, K, HALF), F32),
            pltpu.VMEM((SIDE, K, HALF), F32),
            dma((NB, 3)),
            dma((NF,)), dma((NF,)), dma((NF,)), dma((NF,)),
            dma((2, SIDE)), dma((2, SIDE)),
            dma((SIDE, SIDE)), dma((SIDE, SIDE)),
            dma((SIDE, SIDE)), dma((SIDE, SIDE)),
            dma((SIDE,)), dma((SIDE,)), dma((SIDE,)), dma((SIDE,)),
        ],
        compiler_params=pltpu.CompilerParams(
            collective_id=0, has_side_effects=True, vmem_limit_bytes=40 * 2**20
        ),
        cost_estimate=pl.CostEstimate(
            flops=4 * ROWS * K * NB * W, bytes_accessed=10 * 2**20, transcendentals=0
        ),
    )(samples, components, row_counts, observed, block_owner)


def solution(mesh):
    in_specs = (P("silo", "feat"), P(None, "feat"), P("silo"), P("silo", "feat"), P("feat"))
    out_specs = P(None, ("silo", "feat"))
    return jax.shard_map(local, mesh=mesh, in_specs=in_specs, out_specs=out_specs, check_vma=False)
```

time: 271 us -> 55 us (0.20)
  the two profiles are of different devices: /device:TPU:32 before, /device:TPU:1 now
where the time goes in v1:
time: 55 us; the launch traced here: 54.8 us
  Pallas kernels  47.6 us (87%)
  local copies, waits for them, and re-layouts  6.57 us (12%)
  between operations  0.67 us (1%)
    pallas_call x1, Pallas kernels, local(): pl.pallas_call(kernel, name='pca_grad', out_shape=jax.ShapeDtypeStruct((K...  47.6 us
    unnamed x9, local copies, waits for them, and re-layouts  6.57 us

profile of v1, /device:TPU:1, one launch (start us, length us, event | category | flops | bytes accessed | tf_op | source)
XLA Modules:
  0.0 54.8 jit_solution(13743852603478008560)
XLA Ops:
  0.7 0.0 copy-start
  0.7 3.4 %copy-done = bf16[512,8192]{1,0:T(8,128)(2,1)S(1)} copy-done((bf16[512,8192]{1,0:T(8,128)(2,1)S(1)}, bf16[512,8192]{1,0:T(8,128)(2,1)}, u32[]{:S(2)}) %copy-start) | copy-done | bytes 8388632
  4.0 0.0 copy-start.1
  4.0 1.2 %copy-done.1 = bf16[64,8192]{1,0:T(8,128)(2,1)S(1)} copy-done((bf16[64,8192]{1,0:T(8,128)(2,1)S(1)}, bf16[64,8192]{1,0:T(8,128)(2,1)}, u32[]{:S(2)}) %copy-start.1) | copy-done | bytes 1048600
  5.3 0.0 copy-start.2
  5.3 0.7 %copy-done.2 = s32[1,16]{1,0:T(1,128)S(1)} copy-done((s32[1,16]{1,0:T(1,128)S(1)}, s32[1,16]{1,0:T(1,128)}, u32[]{:S(2)}) %copy-start.2) | copy-done | bytes 88
  5.9 0.0 copy-start.3
  5.9 0.7 %copy-done.3 = s32[16]{0:T(128)S(1)} copy-done((s32[16]{0:T(128)S(1)}, s32[16]{0:T(128)}, u32[]{:S(2)}) %copy-start.3) | copy-done | bytes 88
  6.6 47.6 %pca_grad.1 = f32[64,512]{1,0:T(8,128)S(1)} custom-call(bf16[512,8192]{1,0:T(8,128)(2,1)S(1)} %copy-done, bf16[64,8192]{1,0:T(8,128)(2,1)S(1)} %copy-done.1, s32[1]{0:T(128)S(6)} %copy.7.counts, s32[1,16]{1,0:T(1,128)S(1)} %copy-done.2, s32[16]{0:T(128)S(1)} %copy-done.3), custom_call_target="tpu_custom_call" | custom-call | flops 1073741824 | bytes 10485760 | tf_op jit(solution)/shard_map/pca_grad/pallas_call | solution.py:283
  54.2 0.7 %copy.8 = f32[64,512]{1,0:T(8,128)} copy(f32[64,512]{1,0:T(8,128)S(1)} %pca_grad.1) | data formatting | bytes 262144
Async XLA Ops:
  0.7 3.4 %copy-start = (bf16[512,8192]{1,0:T(8,128)(2,1)S(1)}, bf16[512,8192]{1,0:T(8,128)(2,1)}, u32[]{:S(2)}) copy-start(bf16[512,8192]{1,0:T(8,128)(2,1)} %samples.1) | copy-start | bytes 25165828
  4.0 1.2 %copy-start.1 = (bf16[64,8192]{1,0:T(8,128)(2,1)S(1)}, bf16[64,8192]{1,0:T(8,128)(2,1)}, u32[]{:S(2)}) copy-start(bf16[64,8192]{1,0:T(8,128)(2,1)} %components.1) | copy-start | bytes 3145732
  5.3 0.7 %copy-start.2 = (s32[1,16]{1,0:T(1,128)S(1)}, s32[1,16]{1,0:T(1,128)}, u32[]{:S(2)}) copy-start(s32[1,16]{1,0:T(1,128)} %observed.1) | copy-start | bytes 196
  5.9 0.7 %copy-start.3 = (s32[16]{0:T(128)S(1)}, s32[16]{0:T(128)}, u32[]{:S(2)}) copy-start(s32[16]{0:T(128)} %owner.1) | copy-start | bytes 196

commit v2 on v1

v2 whole, which is shorter than its diff:
```python
import jax
import jax.numpy as jnp
from jax import lax
from jax.experimental import pallas as pl
from jax.experimental.pallas import tpu as pltpu
from jax.sharding import PartitionSpec as P

MESH = pl.DeviceIdType.MESH
F32 = jnp.float32
BF16 = jnp.bfloat16
SIDE = 4
NF = 16
NB = 16
W = 512
HALF = 256
ROWS = 512
K = 64
RK = ROWS + K
KC = K // NF
CW = 640
GROUP = 4

FAR_FIRST = [8, 9, 7, 6, 10, 11, 5, 4, 12, 13, 3, 2, 14, 15, 1]
BLOCKS = [
    (2, 2), (3, 2), (2, 3), (1, 2), (2, 1), (0, 2), (2, 0), (3, 1),
    (1, 3), (0, 1), (1, 0), (3, 3), (1, 1), (0, 3), (3, 0), (0, 0),
]
WAY = {2: 1, 1: 1, 3: SIDE - 1, 0: SIDE - 1}


def dot_nt(a, b):
    return lax.dot_general(a, b, (((1,), (1,)), ((), ())), preferred_element_type=F32)


def dot_nn(a, b):
    return jnp.dot(a, b, preferred_element_type=F32)


def split(v, terms):
    out = []
    for _ in range(terms):
        t = v.astype(BF16)
        out.append(t)
        v = v - t.astype(F32)
    return out


def kernel(
    samples, components, counts, observed_in, owner_in, out,
    observed, owner, xv, acc, sbuf, r1, g2, inv, lhs, cnt, cnt_r,
    ta, tb, ra, rb, sa, sb, r2a, r2b,
    in_sem, ld_sem, s1_s, s1_r, s2_s, s2_r, c_s, c_r,
    a_s, a_r, b_s, b_r, a2_s, a2_r, b2_s, b2_r,
):
    silo = lax.axis_index("silo")
    f = lax.axis_index("feat")
    y, x = silo // SIDE, silo % SIDE

    def feat_dev(off):
        return (silo, lax.rem(f + off, NF))

    def silo_dev(dy, dx):
        return (lax.rem(y + dy, SIDE) * SIDE + lax.rem(x + dx, SIDE), f)

    barrier = pltpu.get_barrier_semaphore()
    for off in FAR_FIRST:
        pl.semaphore_signal(barrier, inc=1, device_id=feat_dev(off), device_id_type=MESH)
    for k in range(1, SIDE):
        pl.semaphore_signal(barrier, inc=1, device_id=silo_dev(0, k), device_id_type=MESH)
        pl.semaphore_signal(barrier, inc=1, device_id=silo_dev(k, 0), device_id_type=MESH)

    small = [
        pltpu.make_async_copy(observed_in, observed, in_sem.at[0]),
        pltpu.make_async_copy(owner_in, owner, in_sem.at[1]),
    ]
    for cp in small:
        cp.start()

    def loads(b):
        cols = pl.ds(pl.multiple_of(b * W, W), W)
        return (
            pltpu.make_async_copy(components.at[:, cols], xv.at[b, pl.ds(ROWS, K)], ld_sem.at[b, 0]),
            pltpu.make_async_copy(samples.at[:, cols], xv.at[b, pl.ds(0, ROWS)], ld_sem.at[b, 1]),
        )

    def start_load(b, c):
        for cp in loads(b):
            cp.start()
        return c

    lax.fori_loop(0, NB, start_load, 0)
    acc[...] = jnp.zeros_like(acc)
    cnt[0] = jnp.full((8, 128), counts[0].astype(F32), F32)
    for cp in small:
        cp.wait()

    def project(g, c):
        for j in range(GROUP):
            for cp in loads(g * GROUP + j):
                cp.wait()
        proj, gram = acc[:, 0:ROWS], acc[:, ROWS:RK]
        for j in range(GROUP):
            b = g * GROUP + j
            r = dot_nt(xv[b, ROWS:RK, :], xv[b])
            proj = proj + observed[0, b].astype(F32) * r[:, 0:ROWS]
            gram = gram + r[:, ROWS:RK]
        acc[:, 0:ROWS] = proj
        acc[:, ROWS:RK] = gram
        return c

    lax.fori_loop(0, NB // GROUP, project, 0)

    for j in range(NF):
        sbuf[j] = acc[KC * j : KC * (j + 1), :]

    pl.semaphore_wait(barrier, NF - 1 + 2 * (SIDE - 1))

    def rs_copy(off):
        peer = lax.rem(f + off, NF)
        return pltpu.make_async_remote_copy(
            src_ref=sbuf.at[peer], dst_ref=r1.at[off], send_sem=s1_s.at[off],
            recv_sem=s1_r.at[off], device_id=(silo, peer), device_id_type=MESH,
        )

    for off in FAR_FIRST:
        rs_copy(off).start()

    def cnt_copy(k, stage):
        dev = silo_dev(0, k) if stage == 0 else silo_dev(k, 0)
        return pltpu.make_async_remote_copy(
            src_ref=cnt.at[stage], dst_ref=cnt_r.at[stage, k], send_sem=c_s.at[stage, k],
            recv_sem=c_r.at[stage, k], device_id=dev, device_id_type=MESH,
        )

    for k in range(1, SIDE):
        cnt_copy(k, 0).start()

    def invert(d, c):
        block = jnp.int32(0)
        for b in range(NB):
            block = jnp.where(owner[b] == d, jnp.int32(b), block)
        inv[d] = block
        return c

    lax.fori_loop(0, NB, invert, 0)

    total = sbuf[f]
    for off in reversed(FAR_FIRST):
        rs_copy(off).wait_recv()
        total = total + r1[off]
    g2[f] = total

    def ag_copy(off):
        return pltpu.make_async_remote_copy(
            src_ref=g2.at[f], dst_ref=g2.at[f], send_sem=s2_s.at[off],
            recv_sem=s2_r.at[off], device_id=feat_dev(off), device_id_type=MESH,
        )

    for off in FAR_FIRST:
        ag_copy(off).start()

    for k in range(1, SIDE):
        cnt_copy(k, 0).wait_recv()
    cnt[1] = cnt[0] + cnt_r[0, 1] + cnt_r[0, 2] + cnt_r[0, 3]
    for k in range(1, SIDE):
        cnt_copy(k, 1).start()

    for off in reversed(FAR_FIRST):
        ag_copy(off).wait_recv()

    for j in range(NF):
        acc[KC * j : KC * (j + 1), :] = g2[j]
    row = lax.broadcasted_iota(jnp.int32, (K, ROWS), 1)
    proj = jnp.where(row < counts[0], acc[:, 0:ROWS], 0.0)
    eye = lax.broadcasted_iota(jnp.int32, (K, K), 0) == lax.broadcasted_iota(
        jnp.int32, (K, K), 1
    )
    factor = jnp.where(eye, 2.0, 0.0) - acc[:, ROWS:RK]
    q = dot_nn(jnp.concatenate(split(factor, 3), axis=0), proj.astype(BF16))
    q = q[0:K] + q[K : 2 * K] + q[2 * K : 3 * K]
    q_hi, q_lo = split(q, 2)
    lhs[0, :, 0:ROWS] = jnp.zeros((2 * K, ROWS), BF16)
    lhs[1, 0:K, 0:ROWS] = q_hi
    lhs[1, K : 2 * K, 0:ROWS] = q_lo
    both = jnp.concatenate(split(proj, 2), axis=0)
    cross = dot_nt(both, both)
    cross = (
        cross[0:K, 0:K] + (cross[0:K, K : 2 * K] + cross[K : 2 * K, 0:K])
        + cross[K : 2 * K, K : 2 * K]
    )
    c_hi, c_lo = split(-cross, 2)
    for s in range(2):
        lhs[s, 0:K, ROWS:RK] = c_hi
        lhs[s, K : 2 * K, ROWS:RK] = c_lo

    def a_copy(kind, i):
        way = WAY[i]
        k = (2, SIDE - way, way)[kind]
        to = (way, SIDE - way, way)[kind]
        return pltpu.make_async_remote_copy(
            src_ref=ta.at[k, i], dst_ref=ra.at[kind, i], send_sem=a_s.at[kind, i],
            recv_sem=a_r.at[kind, i], device_id=silo_dev(0, to), device_id_type=MESH,
        )

    def b_copy(kind, i):
        way = WAY[i]
        k = (2, SIDE - way, way)[kind]
        to = (way, SIDE - way, way)[kind]
        return pltpu.make_async_remote_copy(
            src_ref=tb.at[k, i], dst_ref=rb.at[kind, i], send_sem=b_s.at[kind, i],
            recv_sem=b_r.at[kind, i], device_id=silo_dev(to, 0), device_id_type=MESH,
        )

    def kind_of(k, i):
        if k == 2:
            return 0
        return 1 if k == SIDE - WAY[i] else None

    for dy, dx in BLOCKS:
        d = lax.rem(y + dy, SIDE) * SIDE + lax.rem(x + dx, SIDE)
        b = inv[d]
        p = dot_nn(lhs[observed[0, b]], xv[b])
        p = p[0:K] + p[K : 2 * K]
        ta[dx, dy] = p[:, 0:HALF]
        if kind_of(dx, dy) is not None:
            a_copy(kind_of(dx, dy), dy).start()
        tb[dy, dx] = p[:, HALF:W]
        if kind_of(dy, dx) is not None:
            b_copy(kind_of(dy, dx), dx).start()

    for i in (2, 3, 1, 0):
        k = WAY[i]
        a_copy(0, i).wait_recv()
        ta[k, i] += ra[0, i]
        a_copy(2, i).start()
        b_copy(0, i).wait_recv()
        tb[k, i] += rb[0, i]
        b_copy(2, i).start()

    def a2_copy(k):
        return pltpu.make_async_remote_copy(
            src_ref=sa.at[k], dst_ref=r2a.at[k], send_sem=a2_s.at[k],
            recv_sem=a2_r.at[k], device_id=silo_dev(k, 0), device_id_type=MESH,
        )

    def b2_copy(k):
        return pltpu.make_async_remote_copy(
            src_ref=sb.at[k], dst_ref=r2b.at[k], send_sem=b2_s.at[k],
            recv_sem=b2_r.at[k], device_id=silo_dev(0, k), device_id_type=MESH,
        )

    for i in (2, 3, 1, 0):
        a_copy(1, i).wait_recv()
        a_copy(2, i).wait_recv()
        sa[i] = ta[0, i] + ra[1, i] + ra[2, i]
        if i:
            a2_copy(i).start()
        b_copy(1, i).wait_recv()
        b_copy(2, i).wait_recv()
        sb[i] = tb[0, i] + rb[1, i] + rb[2, i]
        if i:
            b2_copy(i).start()

    for k in range(1, SIDE):
        cnt_copy(k, 1).wait_recv()
    rows = cnt[1] + cnt_r[1, 1] + cnt_r[1, 2] + cnt_r[1, 3]
    scale = -2.0 / rows[0:1, 0:1]
    for k in range(1, SIDE):
        a2_copy(k).wait_recv()
        b2_copy(k).wait_recv()
    out[:, 0:HALF] = scale * (sa[0] + r2a[1] + r2a[2] + r2a[3])
    out[:, HALF:W] = scale * (sb[0] + r2b[1] + r2b[2] + r2b[3])

    for off in range(1, NF):
        rs_copy(off).wait_send()
        ag_copy(off).wait_send()
    for k in range(1, SIDE):
        cnt_copy(k, 0).wait_send()
        cnt_copy(k, 1).wait_send()
        a2_copy(k).wait_send()
        b2_copy(k).wait_send()
    for i in range(SIDE):
        for kind in range(3):
            a_copy(kind, i).wait_send()
            b_copy(kind, i).wait_send()


def local(samples, components, row_counts, observed, block_owner):
    dma = pltpu.SemaphoreType.DMA
    samples, components, observed, block_owner = (
        pltpu.with_memory_space_constraint(a, pltpu.HBM)
        for a in (samples, components, observed, block_owner)
    )
    return pl.pallas_call(
        kernel,
        name="pca_grad",
        out_shape=jax.ShapeDtypeStruct((K, W), F32),
        in_specs=[
            pl.BlockSpec(memory_space=pl.ANY),
            pl.BlockSpec(memory_space=pl.ANY),
            pl.BlockSpec(memory_space=pltpu.SMEM),
            pl.BlockSpec(memory_space=pl.ANY),
            pl.BlockSpec(memory_space=pl.ANY),
        ],
        out_specs=pl.BlockSpec(memory_space=pltpu.VMEM),
        scratch_shapes=[
            pltpu.SMEM((1, NB), jnp.int32),
            pltpu.SMEM((NB,), jnp.int32),
            pltpu.VMEM((NB, RK, W), BF16),
            pltpu.VMEM((K, CW), F32),
            pltpu.VMEM((NF, KC, CW), F32),
            pltpu.VMEM((NF, KC, CW), F32),
            pltpu.VMEM((NF, KC, CW), F32),
            pltpu.SMEM((NB,), jnp.int32),
            pltpu.VMEM((2, 2 * K, RK), BF16),
            pltpu.VMEM((2, 8, 128), F32),
            pltpu.VMEM((2, SIDE, 8, 128), F32),
            pltpu.VMEM((SIDE, SIDE, K, HALF), F32),
            pltpu.VMEM((SIDE, SIDE, K, HALF), F32),
            pltpu.VMEM((3, SIDE, K, HALF), F32),
            pltpu.VMEM((3, SIDE, K, HALF), F32),
            pltpu.VMEM((SIDE, K, HALF), F32),
            pltpu.VMEM((SIDE, K, HALF), F32),
            pltpu.VMEM((SIDE, K, HALF), F32),
            pltpu.VMEM((SIDE, K, HALF), F32),
            dma((2,)), dma((NB, 2)),
            dma((NF,)), dma((NF,)), dma((NF,)), dma((NF,)),
            dma((2, SIDE)), dma((2, SIDE)),
            dma((3, SIDE)), dma((3, SIDE)),
            dma((3, SIDE)), dma((3, SIDE)),
            dma((SIDE,)), dma((SIDE,)), dma((SIDE,)), dma((SIDE,)),
        ],
        compiler_params=pltpu.CompilerParams(
            collective_id=0, has_side_effects=True, vmem_limit_bytes=40 * 2**20
        ),
        cost_estimate=pl.CostEstimate(
            flops=4 * ROWS * K * NB * W, bytes_accessed=10 * 2**20, transcendentals=0
        ),
    )(samples, components, row_counts, observed, block_owner)


def solution(mesh):
    in_specs = (P("silo", "feat"), P(None, "feat"), P("silo"), P("silo", "feat"), P("feat"))
    out_specs = P(None, ("silo", "feat"))
    return jax.shard_map(local, mesh=mesh, in_specs=in_specs, out_specs=out_specs, check_vma=False)
```

time: 55 us -> 42.2 us (0.77)
  the two profiles are of different devices: /device:TPU:1 before, /device:TPU:32 now
where the time goes in v2:
time: 42.2 us; the launch traced here: 41.7 us
  Pallas kernels  40.4 us (96%)
  local copies, waits for them, and re-layouts  0.66 us (2%)
  between operations  0.66 us (2%)
    pallas_call x1, Pallas kernels, local(): pl.pallas_call(kernel, name='pca_grad', out_shape=jax.ShapeDtypeStruct((K...  40.4 us

profile of v2, /device:TPU:32, one launch (start us, length us, event | category | flops | bytes accessed | tf_op | source)
XLA Modules:
  0.0 41.7 jit_solution(7273179639781893213)
XLA Ops:
  0.7 40.4 %pca_grad.1 = f32[64,512]{1,0:T(8,128)S(1)} custom-call(bf16[512,8192]{1,0:T(8,128)(2,1)} %samples.1, bf16[64,8192]{1,0:T(8,128)(2,1)} %components.1, s32[1]{0:T(128)S(6)} %copy.7.counts, s32[1,16]{1,0:T(1,128)} %observed_in.1, s32[16]{0:T(128)} %owner_in.1), custom_call_target="tpu_custom_call" | custom-call | flops 1073741824 | bytes 10485760 | tf_op jit(solution)/shard_map/pca_grad/pallas_call | solution.py:294
  41.0 0.7 %copy.8 = f32[64,512]{1,0:T(8,128)} copy(f32[64,512]{1,0:T(8,128)S(1)} %pca_grad.1) | data formatting | bytes 262144

commit v3 on v2

v3 whole, which is shorter than its diff:
```python
import jax
import jax.numpy as jnp
from jax import lax
from jax.experimental import pallas as pl
from jax.experimental.pallas import tpu as pltpu
from jax.sharding import PartitionSpec as P

MESH = pl.DeviceIdType.MESH
F32 = jnp.float32
BF16 = jnp.bfloat16
SIDE = 4
NF = 16
NB = 16
W = 512
HALF = 256
ROWS = 512
K = 64
RK = ROWS + K
KC = K // NF
LANES = (384, 256)
GROUP = 4

FAR_FIRST = [8, 9, 7, 6, 10, 11, 5, 4, 12, 13, 3, 2, 14, 15, 1]
BLOCKS = [
    (2, 2), (3, 2), (2, 3), (1, 2), (2, 1), (0, 2), (2, 0), (3, 1),
    (1, 3), (0, 1), (1, 0), (3, 3), (1, 1), (0, 3), (3, 0), (0, 0),
]
WAY = {2: 1, 1: 1, 3: SIDE - 1, 0: SIDE - 1}


def dot_nt(a, b):
    return lax.dot_general(a, b, (((1,), (1,)), ((), ())), preferred_element_type=F32)


def dot_nn(a, b):
    return jnp.dot(a, b, preferred_element_type=F32)


def split(v, terms):
    out = []
    for _ in range(terms):
        t = v.astype(BF16)
        out.append(t)
        v = v - t.astype(F32)
    return out


def kernel(
    samples, components, counts, observed_in, owner_in, out,
    observed, owner, xs, seen, acc_0, acc_1, sbuf_0, sbuf_1, r1_0, r1_1, g2_0, g2_1, inv, lhs, cnt, cnt_r,
    ta, tb, ra, rb, sa, sb, r2a, r2b,
    in_sem, comp_sem, ld_sem, s1_s, s1_r, s2_s, s2_r, c_s, c_r,
    a_s, a_r, b_s, b_r, a2_s, a2_r, b2_s, b2_r,
):
    acc, sbuf, r1, g2 = (acc_0, acc_1), (sbuf_0, sbuf_1), (r1_0, r1_1), (g2_0, g2_1)
    silo = lax.axis_index("silo")
    f = lax.axis_index("feat")
    y, x = silo // SIDE, silo % SIDE

    def feat_dev(off):
        return (silo, lax.rem(f + off, NF))

    def silo_dev(dy, dx):
        return (lax.rem(y + dy, SIDE) * SIDE + lax.rem(x + dx, SIDE), f)

    small = [
        pltpu.make_async_copy(observed_in, observed, in_sem.at[0]),
        pltpu.make_async_copy(owner_in, owner, in_sem.at[1]),
    ]
    load_comp = pltpu.make_async_copy(components, xs.at[pl.ds(ROWS, K)], comp_sem.at[0])

    def columns(g):
        return pl.ds(pl.multiple_of(g * GROUP * W, GROUP * W), GROUP * W)

    def load(h, g):
        part = (pl.ds(h * HALF, HALF), columns(g))
        return pltpu.make_async_copy(samples.at[part], xs.at[part], ld_sem.at[h, g])

    for cp in small:
        cp.start()
    load_comp.start()
    for g in range(NB // GROUP):
        load(0, g).start()

    barrier = pltpu.get_barrier_semaphore()
    for off in FAR_FIRST:
        pl.semaphore_signal(barrier, inc=1, device_id=feat_dev(off), device_id_type=MESH)
    for k in range(1, SIDE):
        pl.semaphore_signal(barrier, inc=1, device_id=silo_dev(0, k), device_id_type=MESH)
        pl.semaphore_signal(barrier, inc=1, device_id=silo_dev(k, 0), device_id_type=MESH)

    cnt[0] = jnp.full((8, 128), counts[0].astype(F32), F32)
    for cp in small:
        cp.wait()
    load_comp.wait()

    for b in range(NB):
        cols = slice(b * W, (b + 1) * W)
        seen[:, cols] = xs[ROWS:RK, cols] * observed[0, b].astype(F32).astype(BF16)

    def rs_copy(h, off):
        peer = lax.rem(f + off, NF)
        return pltpu.make_async_remote_copy(
            src_ref=sbuf[h].at[peer], dst_ref=r1[h].at[off], send_sem=s1_s.at[h, off],
            recv_sem=s1_r.at[h, off], device_id=(silo, peer), device_id_type=MESH,
        )

    def ag_copy(h, off):
        return pltpu.make_async_remote_copy(
            src_ref=g2[h].at[f], dst_ref=g2[h].at[f], send_sem=s2_s.at[h, off],
            recv_sem=s2_r.at[h, off], device_id=feat_dev(off), device_id_type=MESH,
        )

    acc[0][:, 0:HALF] = jnp.zeros((K, HALF), F32)
    acc[0][:, HALF : HALF + K] = dot_nt(xs[ROWS:RK, :], xs[ROWS:RK, :])
    acc[1][...] = jnp.zeros((K, HALF), F32)
    for h in range(2):

        def project(g, c):
            load(h, g).wait()
            if h == 0:
                load(1, g).start()
            acc[h][:, 0:HALF] += dot_nt(
                seen[:, columns(g)], xs[h * HALF : (h + 1) * HALF, columns(g)]
            )
            return c

        lax.fori_loop(0, NB // GROUP, project, 0)
        for j in range(NF):
            sbuf[h][j] = acc[h][KC * j : KC * (j + 1), :]
        if h == 0:
            pl.semaphore_wait(barrier, NF - 1 + 2 * (SIDE - 1))
        for off in FAR_FIRST:
            rs_copy(h, off).start()

    def cnt_copy(k, stage):
        dev = silo_dev(0, k) if stage == 0 else silo_dev(k, 0)
        return pltpu.make_async_remote_copy(
            src_ref=cnt.at[stage], dst_ref=cnt_r.at[stage, k], send_sem=c_s.at[stage, k],
            recv_sem=c_r.at[stage, k], device_id=dev, device_id_type=MESH,
        )

    for k in range(1, SIDE):
        cnt_copy(k, 0).start()

    def invert(d, c):
        block = jnp.int32(0)
        for b in range(NB):
            block = jnp.where(owner[b] == d, jnp.int32(b), block)
        inv[d] = block
        return c

    lax.fori_loop(0, NB, invert, 0)

    for h in range(2):
        total = sbuf[h][f]
        for off in reversed(FAR_FIRST):
            rs_copy(h, off).wait_recv()
            total = total + r1[h][off]
        g2[h][f] = total
        for off in FAR_FIRST:
            ag_copy(h, off).start()

    for k in range(1, SIDE):
        cnt_copy(k, 0).wait_recv()
    cnt[1] = cnt[0] + cnt_r[0, 1] + cnt_r[0, 2] + cnt_r[0, 3]
    for k in range(1, SIDE):
        cnt_copy(k, 1).start()

    lhs[0, :, 0:ROWS] = jnp.zeros((2 * K, ROWS), BF16)
    cross = jnp.zeros((2 * K, 2 * K), F32)
    for h in range(2):
        for off in reversed(FAR_FIRST):
            ag_copy(h, off).wait_recv()
        for j in range(NF):
            acc[h][KC * j : KC * (j + 1), :] = g2[h][j]
        if h == 0:
            eye = lax.broadcasted_iota(jnp.int32, (K, K), 0) == lax.broadcasted_iota(
                jnp.int32, (K, K), 1
            )
            factor = jnp.where(eye, 2.0, 0.0) - acc[0][:, HALF : HALF + K]
            factor = jnp.concatenate(split(factor, 3), axis=0)
        row = lax.broadcasted_iota(jnp.int32, (K, HALF), 1) + h * HALF
        proj = jnp.where(row < counts[0], acc[h][:, 0:HALF], 0.0)
        both = split(proj, 2)
        q = dot_nn(factor, both[0])
        q_hi, q_lo = split(q[0:K] + q[K : 2 * K] + q[2 * K : 3 * K], 2)
        lhs[1, 0:K, h * HALF : (h + 1) * HALF] = q_hi
        lhs[1, K : 2 * K, h * HALF : (h + 1) * HALF] = q_lo
        both = jnp.concatenate(both, axis=0)
        cross = cross + dot_nt(both, both)
    cross = (
        cross[0:K, 0:K] + (cross[0:K, K : 2 * K] + cross[K : 2 * K, 0:K])
        + cross[K : 2 * K, K : 2 * K]
    )
    c_hi, c_lo = split(-cross, 2)
    for s in range(2):
        lhs[s, 0:K, ROWS:RK] = c_hi
        lhs[s, K : 2 * K, ROWS:RK] = c_lo

    def a_copy(kind, i):
        way = WAY[i]
        k = (2, SIDE - way, way)[kind]
        to = (way, SIDE - way, way)[kind]
        return pltpu.make_async_remote_copy(
            src_ref=ta.at[k, i], dst_ref=ra.at[kind, i], send_sem=a_s.at[kind, i],
            recv_sem=a_r.at[kind, i], device_id=silo_dev(0, to), device_id_type=MESH,
        )

    def b_copy(kind, i):
        way = WAY[i]
        k = (2, SIDE - way, way)[kind]
        to = (way, SIDE - way, way)[kind]
        return pltpu.make_async_remote_copy(
            src_ref=tb.at[k, i], dst_ref=rb.at[kind, i], send_sem=b_s.at[kind, i],
            recv_sem=b_r.at[kind, i], device_id=silo_dev(to, 0), device_id_type=MESH,
        )

    def kind_of(k, i):
        if k == 2:
            return 0
        return None

    for dy, dx in BLOCKS:
        d = lax.rem(y + dy, SIDE) * SIDE + lax.rem(x + dx, SIDE)
        b = inv[d]
        cols = pl.ds(b * W, W)
        p = dot_nn(lhs[observed[0, b]], xs[:, cols])
        p = p[0:K] + p[K : 2 * K]
        ta[dx, dy] = p[:, 0:HALF]
        if kind_of(dx, dy) is not None:
            a_copy(kind_of(dx, dy), dy).start()
        tb[dy, dx] = p[:, HALF:W]
        if kind_of(dy, dx) is not None:
            b_copy(kind_of(dy, dx), dx).start()

    for i in (2, 3):
        a_copy(0, i).wait_send()
        b_copy(0, i).wait_send()
        a_copy(1, 5 - i).start()
        b_copy(1, 5 - i).start()
    for i in (0, 1):
        a_copy(0, i).wait_send()
        b_copy(0, i).wait_send()
    a_copy(1, 1).start()
    b_copy(1, 1).start()
    for i in (2, 3, 1, 0):
        k = WAY[i]
        a_copy(0, i).wait_recv()
        ta[k, i] += ra[0, i]
        a_copy(2, i).start()
        b_copy(0, i).wait_recv()
        tb[k, i] += rb[0, i]
        b_copy(2, i).start()
    a_copy(1, 0).start()
    b_copy(1, 0).start()

    for h in range(2):
        for off in range(1, NF):
            rs_copy(h, off).wait_send()
            ag_copy(h, off).wait_send()
    for k in range(1, SIDE):
        cnt_copy(k, 0).wait_send()
        cnt_copy(k, 1).wait_send()
        cnt_copy(k, 1).wait_recv()
    rows = cnt[1] + cnt_r[1, 1] + cnt_r[1, 2] + cnt_r[1, 3]
    scale = -2.0 / rows[0:1, 0:1]

    def a2_copy(k):
        return pltpu.make_async_remote_copy(
            src_ref=sa.at[k], dst_ref=r2a.at[k], send_sem=a2_s.at[k],
            recv_sem=a2_r.at[k], device_id=silo_dev(k, 0), device_id_type=MESH,
        )

    def b2_copy(k):
        return pltpu.make_async_remote_copy(
            src_ref=sb.at[k], dst_ref=r2b.at[k], send_sem=b2_s.at[k],
            recv_sem=b2_r.at[k], device_id=silo_dev(0, k), device_id_type=MESH,
        )

    for i in (2, 1, 3, 0):
        a_copy(1, i).wait_recv()
        a_copy(2, i).wait_recv()
        sa[i] = ta[0, i] + ra[1, i] + ra[2, i]
        if i:
            a2_copy(i).start()
        b_copy(1, i).wait_recv()
        b_copy(2, i).wait_recv()
        sb[i] = tb[0, i] + rb[1, i] + rb[2, i]
        if i:
            b2_copy(i).start()

    for i in range(SIDE):
        for kind in range(1, 3):
            a_copy(kind, i).wait_send()
            b_copy(kind, i).wait_send()
    for k in (1, 3, 2):
        a2_copy(k).wait_recv()
        b2_copy(k).wait_recv()
    out[:, 0:HALF] = scale * (sa[0] + r2a[1] + r2a[2] + r2a[3])
    out[:, HALF:W] = scale * (sb[0] + r2b[1] + r2b[2] + r2b[3])

    for k in range(1, SIDE):
        a2_copy(k).wait_send()
        b2_copy(k).wait_send()


def local(samples, components, row_counts, observed, block_owner):
    dma = pltpu.SemaphoreType.DMA
    samples, components, observed, block_owner = (
        pltpu.with_memory_space_constraint(a, pltpu.HBM)
        for a in (samples, components, observed, block_owner)
    )
    return pl.pallas_call(
        kernel,
        name="pca_grad",
        out_shape=jax.ShapeDtypeStruct((K, W), F32),
        in_specs=[
            pl.BlockSpec(memory_space=pl.ANY),
            pl.BlockSpec(memory_space=pl.ANY),
            pl.BlockSpec(memory_space=pltpu.SMEM),
            pl.BlockSpec(memory_space=pl.ANY),
            pl.BlockSpec(memory_space=pl.ANY),
        ],
        out_specs=pl.BlockSpec(memory_space=pltpu.VMEM),
        scratch_shapes=[
            pltpu.SMEM((1, NB), jnp.int32),
            pltpu.SMEM((NB,), jnp.int32),
            pltpu.VMEM((RK, NB * W), BF16),
            pltpu.VMEM((K, NB * W), BF16),
            pltpu.VMEM((K, LANES[0]), F32),
            pltpu.VMEM((K, LANES[1]), F32),
            pltpu.VMEM((NF, KC, LANES[0]), F32),
            pltpu.VMEM((NF, KC, LANES[1]), F32),
            pltpu.VMEM((NF, KC, LANES[0]), F32),
            pltpu.VMEM((NF, KC, LANES[1]), F32),
            pltpu.VMEM((NF, KC, LANES[0]), F32),
            pltpu.VMEM((NF, KC, LANES[1]), F32),
            pltpu.SMEM((NB,), jnp.int32),
            pltpu.VMEM((2, 2 * K, RK), BF16),
            pltpu.VMEM((2, 8, 128), F32),
            pltpu.VMEM((2, SIDE, 8, 128), F32),
            pltpu.VMEM((SIDE, SIDE, K, HALF), F32),
            pltpu.VMEM((SIDE, SIDE, K, HALF), F32),
            pltpu.VMEM((3, SIDE, K, HALF), F32),
            pltpu.VMEM((3, SIDE, K, HALF), F32),
            pltpu.VMEM((SIDE, K, HALF), F32),
            pltpu.VMEM((SIDE, K, HALF), F32),
            pltpu.VMEM((SIDE, K, HALF), F32),
            pltpu.VMEM((SIDE, K, HALF), F32),
            dma((2,)), dma((1,)), dma((2, NB // GROUP)),
            dma((2, NF)), dma((2, NF)), dma((2, NF)), dma((2, NF)),
            dma((2, SIDE)), dma((2, SIDE)),
            dma((3, SIDE)), dma((3, SIDE)),
            dma((3, SIDE)), dma((3, SIDE)),
            dma((SIDE,)), dma((SIDE,)), dma((SIDE,)), dma((SIDE,)),
        ],
        compiler_params=pltpu.CompilerParams(
            collective_id=0, has_side_effects=True, vmem_limit_bytes=40 * 2**20
        ),
        cost_estimate=pl.CostEstimate(
            flops=4 * ROWS * K * NB * W, bytes_accessed=10 * 2**20, transcendentals=0
        ),
    )(samples, components, row_counts, observed, block_owner)


def solution(mesh):
    in_specs = (P("silo", "feat"), P(None, "feat"), P("silo"), P("silo", "feat"), P("feat"))
    out_specs = P(None, ("silo", "feat"))
    return jax.shard_map(local, mesh=mesh, in_specs=in_specs, out_specs=out_specs, check_vma=False)
```

time: 42.2 us -> 39.2 us (0.929); the launches traced: 41.7 us -> 39.1 us
  Pallas kernels: 40.4 us -> 37.8 us
    pallas_call x1, Pallas kernels: 40.4 us -> 37.8 us  [local(): pl.pallas_call(kernel, name='pca_grad', out_shape=jax.ShapeDtypeStruct((K...]
where the time goes in v3:
time: 39.2 us; the launch traced here: 39.1 us
  Pallas kernels  37.8 us (96%)
  local copies, waits for them, and re-layouts  0.66 us (2%)
  between operations  0.66 us (2%)
    pallas_call x1, Pallas kernels, local(): pl.pallas_call(kernel, name='pca_grad', out_shape=jax.ShapeDtypeStruct((K...  37.8 us

profile of v3, /device:TPU:32, one launch (start us, length us, event | category | flops | bytes accessed | tf_op | source)
XLA Modules:
  0.0 39.1 jit_solution(1343070996863373285)
XLA Ops:
  0.7 37.8 %pca_grad.1 = f32[64,512]{1,0:T(8,128)S(1)} custom-call(bf16[512,8192]{1,0:T(8,128)(2,1)} %samples.1, bf16[64,8192]{1,0:T(8,128)(2,1)} %components.1, s32[1]{0:T(128)S(6)} %copy.7.counts, s32[1,16]{1,0:T(1,128)} %observed_in.1, s32[16]{0:T(128)} %owner_in.1), custom_call_target="tpu_custom_call" | custom-call | flops 1073741824 | bytes 10485760 | tf_op jit(solution)/shard_map/pca_grad/pallas_call | solution.py:314
  38.4 0.7 %copy.8 = f32[64,512]{1,0:T(8,128)} copy(f32[64,512]{1,0:T(8,128)S(1)} %pca_grad.1) | data formatting | bytes 262144

commit v4 on v3

--- a/solution.py
+++ b/solution.py
@@ -18,7 +18,7 @@
 RK = ROWS + K
 KC = K // NF
 LANES = (384, 256)
-GROUP = 4
+GROUP = 8
 
 FAR_FIRST = [8, 9, 7, 6, 10, 11, 5, 4, 12, 13, 3, 2, 14, 15, 1]
 BLOCKS = [
@@ -81,6 +81,8 @@
     load_comp.start()
     for g in range(NB // GROUP):
         load(0, g).start()
+    for g in range(NB // GROUP):
+        load(1, g).start()
 
     barrier = pltpu.get_barrier_semaphore()
     for off in FAR_FIRST:
@@ -118,8 +120,6 @@
 
         def project(g, c):
             load(h, g).wait()
-            if h == 0:
-                load(1, g).start()
             acc[h][:, 0:HALF] += dot_nt(
                 seen[:, columns(g)], xs[h * HALF : (h + 1) * HALF, columns(g)]
             )
@@ -168,7 +168,7 @@
         cnt_copy(k, 1).start()
 
     lhs[0, :, 0:ROWS] = jnp.zeros((2 * K, ROWS), BF16)
-    cross = jnp.zeros((2 * K, 2 * K), F32)
+    cross = jnp.zeros((K, K), F32)
     for h in range(2):
         for off in reversed(FAR_FIRST):
             ag_copy(h, off).wait_recv()
@@ -179,20 +179,17 @@
                 jnp.int32, (K, K), 1
             )
             factor = jnp.where(eye, 2.0, 0.0) - acc[0][:, HALF : HALF + K]
-            factor = jnp.concatenate(split(factor, 3), axis=0)
+            factor = jnp.concatenate(split(factor, 3), axis=1)
         row = lax.broadcasted_iota(jnp.int32, (K, HALF), 1) + h * HALF
         proj = jnp.where(row < counts[0], acc[h][:, 0:HALF], 0.0)
-        both = split(proj, 2)
-        q = dot_nn(factor, both[0])
-        q_hi, q_lo = split(q[0:K] + q[K : 2 * K] + q[2 * K : 3 * K], 2)
+        hi, lo = split(proj, 2)
+        q = dot_nn(factor, jnp.concatenate([hi, hi, hi], axis=0))
+        q_hi, q_lo = split(q, 2)
         lhs[1, 0:K, h * HALF : (h + 1) * HALF] = q_hi
         lhs[1, K : 2 * K, h * HALF : (h + 1) * HALF] = q_lo
-        both = jnp.concatenate(both, axis=0)
-        cross = cross + dot_nt(both, both)
-    cross = (
-        cross[0:K, 0:K] + (cross[0:K, K : 2 * K] + cross[K : 2 * K, 0:K])
-        + cross[K : 2 * K, K : 2 * K]
-    )
+        cross = cross + dot_nt(
+            jnp.concatenate([hi, hi, lo, lo], axis=1), jnp.concatenate([hi, lo, hi, lo], axis=1)
+        )
     c_hi, c_lo = split(-cross, 2)
     for s in range(2):
         lhs[s, 0:K, ROWS:RK] = c_hi
@@ -216,44 +213,43 @@
             recv_sem=b_r.at[kind, i], device_id=silo_dev(to, 0), device_id_type=MESH,
         )
 
-    def kind_of(k, i):
-        if k == 2:
-            return 0
-        return None
+    def send(kind, *rows):
+        for i in rows:
+            a_copy(kind, i).start()
+            b_copy(kind, i).start()
+
+    def sent(kind, *rows):
+        for i in rows:
+            a_copy(kind, i).wait_send()
+            b_copy(kind, i).wait_send()
+
+    def relay(*rows):
+        for i in rows:
+            k = WAY[i]
+            a_copy(0, i).wait_recv()
+            ta[k, i] += ra[0, i]
+            a_copy(2, i).start()
+            b_copy(0, i).wait_recv()
+            tb[k, i] += rb[0, i]
+            b_copy(2, i).start()
 
     for dy, dx in BLOCKS:
         d = lax.rem(y + dy, SIDE) * SIDE + lax.rem(x + dx, SIDE)
         b = inv[d]
-        cols = pl.ds(b * W, W)
-        p = dot_nn(lhs[observed[0, b]], xs[:, cols])
+        p = dot_nn(lhs[observed[0, b]], xs[:, pl.ds(b * W, W)])
         p = p[0:K] + p[K : 2 * K]
         ta[dx, dy] = p[:, 0:HALF]
-        if kind_of(dx, dy) is not None:
-            a_copy(kind_of(dx, dy), dy).start()
         tb[dy, dx] = p[:, HALF:W]
-        if kind_of(dy, dx) is not None:
-            b_copy(kind_of(dy, dx), dx).start()
-
-    for i in (2, 3):
-        a_copy(0, i).wait_send()
-        b_copy(0, i).wait_send()
-        a_copy(1, 5 - i).start()
-        b_copy(1, 5 - i).start()
-    for i in (0, 1):
-        a_copy(0, i).wait_send()
-        b_copy(0, i).wait_send()
-    a_copy(1, 1).start()
-    b_copy(1, 1).start()
-    for i in (2, 3, 1, 0):
-        k = WAY[i]
-        a_copy(0, i).wait_recv()
-        ta[k, i] += ra[0, i]
-        a_copy(2, i).start()
-        b_copy(0, i).wait_recv()
-        tb[k, i] += rb[0, i]
-        b_copy(2, i).start()
-    a_copy(1, 0).start()
-    b_copy(1, 0).start()
+        if dx == 2 and dy in (2, 3, 1, 0):
+            a_copy(0, dy).start()
+        if dy == 2 and dx in (2, 3, 1, 0):
+            b_copy(0, dx).start()
+    send(1, 3, 2)
+    sent(0, 2, 3)
+    sent(0, 1, 0)
+    send(1, 1)
+    relay(2, 3, 1, 0)
+    send(1, 0)
 
     for h in range(2):
         for off in range(1, NF):
@@ -278,7 +274,7 @@
             recv_sem=b2_r.at[k], device_id=silo_dev(0, k), device_id_type=MESH,
         )
 
-    for i in (2, 1, 3, 0):
+    def first_sum(i):
         a_copy(1, i).wait_recv()
         a_copy(2, i).wait_recv()
         sa[i] = ta[0, i] + ra[1, i] + ra[2, i]
@@ -290,10 +286,13 @@
         if i:
             b2_copy(i).start()
 
-    for i in range(SIDE):
-        for kind in range(1, 3):
-            a_copy(kind, i).wait_send()
-            b_copy(kind, i).wait_send()
+    first_sum(2)
+    first_sum(3)
+    first_sum(1)
+    first_sum(0)
+
+    sent(1, 0, 1, 2, 3)
+    sent(2, 0, 1, 2, 3)
     for k in (1, 3, 2):
         a2_copy(k).wait_recv()
         b2_copy(k).wait_recv()

time: 39.2 us -> 39 us (level)
  no operation moved by 1% of the time
where the time goes in v4:
time: 39 us; the launch traced here: 38.9 us
  Pallas kernels  37.6 us (96%)
  local copies, waits for them, and re-layouts  0.66 us (2%)
  between operations  0.66 us (2%)
    pallas_call x1, Pallas kernels, local(): pl.pallas_call(kernel, name='pca_grad', out_shape=jax.ShapeDtypeStruct((K...  37.6 us

profile of v4, /device:TPU:32, one launch (start us, length us, event | category | flops | bytes accessed | tf_op | source)
XLA Modules:
  0.0 38.9 jit_solution(13852637871431729894)
XLA Ops:
  0.7 37.6 %pca_grad.1 = f32[64,512]{1,0:T(8,128)S(1)} custom-call(bf16[512,8192]{1,0:T(8,128)(2,1)} %samples.1, bf16[64,8192]{1,0:T(8,128)(2,1)} %components.1, s32[1]{0:T(128)S(6)} %copy.7.counts, s32[1,16]{1,0:T(1,128)} %observed_in.1, s32[16]{0:T(128)} %owner_in.1), custom_call_target="tpu_custom_call" | custom-call | flops 1073741824 | bytes 10485760 | tf_op jit(solution)/shard_map/pca_grad/pallas_call | solution.py:313
  38.2 0.7 %copy.8 = f32[64,512]{1,0:T(8,128)} copy(f32[64,512]{1,0:T(8,128)S(1)} %pca_grad.1) | data formatting | bytes 262144
